TPU v7x, 128 devices: a whole 4x4x4 slice. The times are simulated.
128 devices in a mesh: horiz: 16 (over z, y), depth: 8 (over x, core).
Axes of the slice: x: 4, y: 4, z: 4, core: 2. Of those that a mesh axis runs over, the one named last changes fastest.
Arguments:
- source_field: float32 [64, 512, 512], P('depth', 'horiz'), may hold values from -6 to 6
- methane: float32 [64, 512, 512], P('depth', 'horiz'), may hold values from 0.2 to 1.5
- sulfate: float32 [64, 512, 512], P('depth', 'horiz'), may hold values from 0.2 to 1.5
- layer_of_cell: int32 [64], replicated, may hold values from 0 to 7
- perm_horizontal: float32 [8], replicated, may hold values from 0.3 to 3
- perm_vertical: float32 [8], replicated, may hold values from 0.3 to 3
- vent_mask: int32 [512, 512], P('horiz'), may hold values 0 or 1
Outputs:
- pressure: float32 [64, 512, 512], P('depth', 'horiz')
- methane_out: float32 [64, 512, 512], P('depth', 'horiz')
- sulfate_out: float32 [64, 512, 512], P('depth', 'horiz')
All inputs are finite; a program needn't handle non-finite values. No bound on the sum of `vent_mask` on one device may be relied on, other than what follows from the above.
Results may differ from a plain program's by a relative error of at most 0.0003.
Values sent between devices are 32-bit elements; how exact they have to be, the bound alone decides.
A program may use at most 64 MiB of HBM per device.

v0:
```python
import jax
import jax.numpy as jnp
import ml_dtypes
import numpy as np
from jax import lax
from jax.experimental import pallas as pl
from jax.experimental.pallas import tpu as pltpu
from jax.sharding import PartitionSpec as P

STEPS = 4
STORAGE = 0.004
COURANT = 0.5
REACTION = 4.0
VENT_INPUT = 4.0

NZ = 64
N = 512
NH = 16
ND = 8
ZL = 8
XL = 32
HALO = 4
ZE = ZL + 2 * HALO
XE = XL + 2 * HALO
NX_CHIPS = 4
ZB = NZ // NX_CHIPS
NQ = 2 * NH

PLANE = sorted(
    [(z, y, c) for z in range(4) for y in range(4) for c in range(2)][1:],
    key=lambda o: -(min(o[0], 4 - o[0]) + min(o[1], 4 - o[1])))

PARTS = 2

F32 = jnp.float32
BF16 = jnp.bfloat16


def tables():
    k = np.arange(N)
    angle = (k[:, None] * k[None, :] % N) * (2.0 * np.pi / N)
    cas = np.cos(angle) + np.sin(angle)
    hi = cas.astype(np.float32).astype(ml_dtypes.bfloat16)
    lo = (cas - hi.astype(np.float64)).astype(np.float32).astype(ml_dtypes.bfloat16)
    eig = (4.0 * np.sin(np.pi * k / N) ** 2).astype(np.float32)
    eig_x = np.broadcast_to(eig.reshape(1, N), (16, N)).copy()
    eig_y = np.broadcast_to(eig.reshape(NQ, 16, 1), (NQ, 16, 128)).copy()
    return hi, lo, eig_x, eig_y


def split(v):
    hi = v.astype(BF16)
    return hi, (v - hi.astype(F32)).astype(BF16)


def dot3(a, b, dims=((1,), (0,))):
    (ah, al), (bh, bl) = a, b
    d = lambda x, y: lax.dot_general(x, y, (dims, ((), ())), preferred_element_type=F32)
    return d(ah, bh) + (d(al, bh) + d(ah, bl))


def kernel(
    src_in, met, sul, layer, ph, pv, vent_in, hhi_in, hlo_in, eig_x_in, eig_y,
    out_p, out_m, out_s,
    src, vent, hhi, hlo, eig_x, res_m, res_s,
    y1, r1, ah, al, fz, w1, y4, ey,
    inv_d, inv_u, prod_d, prod_u, gd, pi, send_a, recv_a,
    ep, em, es, em2, es2, ev, vin, pack, xin, coef, tend, curve,
    mx, mxh, mxd, cpl, khs,
    s1, q1, s2, q2, s4, q4, hs, hq, vs, vq, ms, mq, ns, nq, lsem,
):
    h = lax.axis_index("horiz")
    d = lax.axis_index("depth")
    chip = lax.div(d, 2)
    core = lax.rem(d, 2)
    q = h * 2 + core

    drains = {}

    def dev(hh, dd):
        return {"horiz": hh, "depth": dd}

    def mate(j):
        return lax.rem(h + j, NH)

    hz, hy = lax.div(h, 4), lax.rem(h, 4)

    def fellow(j, sign=1):
        dz, dy, dc = PLANE[j]
        fh = lax.rem(hz + sign * dz + 4, 4) * 4 + lax.rem(hy + sign * dy + 4, 4)
        fc = lax.rem(core + dc, 2)
        return 2 * fh + fc, fh, fc

    def slot(oq):
        return lax.rem(oq, 2) * NH + lax.div(oq, 2)

    h_up, h_dn = lax.rem(h + 1, NH), lax.rem(h + NH - 1, NH)
    d_up, d_dn = lax.rem(d + 1, ND), lax.rem(d + ND - 1, ND)

    first_loads = [
        pltpu.make_async_copy(src_in, src, lsem.at[3]),
        pltpu.make_async_copy(hhi_in, hhi, lsem.at[4]),
        pltpu.make_async_copy(hlo_in, hlo, lsem.at[5]),
    ]
    for c in first_loads:
        c.start()

    barrier = pltpu.get_barrier_semaphore()

    for j in range(NQ - 1):
        _, fh, fc = fellow(j)
        pl.semaphore_signal(barrier, inc=1, device_id=dev(fh, 2 * chip + fc))

    def greet_d(j, _):
        pl.semaphore_signal(barrier, inc=1, device_id=dev(h, lax.rem(d + j, ND)))
        return 0

    lax.fori_loop(1, ND, greet_d, 0)
    for hh in (h_up, h_dn):
        for dd in (d_up, d_dn):
            pl.semaphore_signal(barrier, inc=1, device_id=dev(hh, dd))

    own_copies = [
        pltpu.make_async_copy(met, em.at[pl.ds(HALO, ZL), pl.ds(0, XL)], lsem.at[0]),
        pltpu.make_async_copy(sul, es.at[pl.ds(HALO, ZL), pl.ds(0, XL)], lsem.at[1]),
        pltpu.make_async_copy(eig_y.at[q], ey, lsem.at[2]),
        pltpu.make_async_copy(vent_in, vent, lsem.at[6]),
        pltpu.make_async_copy(eig_x_in, eig_x, lsem.at[7]),
    ]
    for c in own_copies:
        c.start()
    drains["own"] = lambda: [c.wait() for c in own_copies]

    for c in first_loads:
        c.wait()
    s = split(src[...].reshape(ZL * XL, N))
    for n in range(2):
        rows = (hhi[256 * n:256 * n + 256], hlo[256 * n:256 * n + 256])
        y1[16 * n:16 * n + 16] = dot3(rows, s, ((1,), (1,))).reshape(16, 16, ZL * XL)

    pl.semaphore_wait(barrier, (NQ - 1) + (ND - 1) + 4)

    def copy1(j, oq):
        pq, fh, fc = fellow(j)
        return pltpu.make_async_remote_copy(
            src_ref=y1.at[pq], dst_ref=r1.at[slot(oq)],
            send_sem=s1.at[j], recv_sem=q1.at[j], device_id=dev(fh, 2 * chip + fc))

    def go1():
        for j in range(NQ - 1):
            copy1(j, q).start()

    go1()
    def left1():
        for j in range(NQ - 1):
            copy1(j, q).wait_send()
    drains["1"] = left1

    def halo_copies(f, ref, dirs):
        own = pl.ds(0, XL)
        lo_p, hi_p = pack.at[f, 0], pack.at[f, 1]
        plan = (
            (ref.at[pl.ds(8, 4), own], ref.at[pl.ds(0, 4), own], h, d_up),
            (ref.at[pl.ds(4, 4), own], ref.at[pl.ds(12, 4), own], h, d_dn),
            (hi_p, xin.at[f, 0, pl.ds(2, 4)], h_up, d),
            (lo_p, xin.at[f, 1, pl.ds(2, 4)], h_dn, d),
            (hi_p.at[pl.ds(2, 2)], xin.at[f, 0, pl.ds(0, 2)], h_up, d_up),
            (hi_p.at[pl.ds(0, 2)], xin.at[f, 0, pl.ds(6, 2)], h_up, d_dn),
            (lo_p.at[pl.ds(2, 2)], xin.at[f, 1, pl.ds(0, 2)], h_dn, d_up),
            (lo_p.at[pl.ds(0, 2)], xin.at[f, 1, pl.ds(6, 2)], h_dn, d_dn),
            (ref.at[pl.ds(11, 1), own], ref.at[pl.ds(3, 1), own], h, d_up),
            (ref.at[pl.ds(4, 1), own], ref.at[pl.ds(12, 1), own], h, d_dn),
            (ref.at[pl.ds(8, 3), own], ref.at[pl.ds(0, 3), own], h, d_up),
            (ref.at[pl.ds(5, 3), own], ref.at[pl.ds(13, 3), own], h, d_dn),
        )
        return [
            pltpu.make_async_remote_copy(
                src_ref=plan[i][0], dst_ref=plan[i][1], send_sem=hs.at[f, i], recv_sem=hq.at[f, i],
                device_id=dev(plan[i][2], plan[i][3]))
            for i in dirs
        ]

    sub8 = lax.broadcasted_iota(jnp.int32, (8, N), 0)

    def pack_rows(f, ref):
        for zz in range(ZL // 2):
            even, odd = ref[HALO + 2 * zz], ref[HALO + 2 * zz + 1]
            pack[f, 0, zz] = jnp.where(sub8 < 4, even[0:8], pltpu.roll(odd[0:8], 4, 0))
            pack[f, 1, zz] = jnp.where(sub8 >= 4, even[24:32], pltpu.roll(odd[24:32], 4, 0))

    def unpack_rows(f, ref, pairs=range(ZE // 2)):
        for zz in pairs:
            lower, upper = xin[f, 0, zz], xin[f, 1, zz]
            ref[2 * zz, XL:XE] = jnp.where(sub8 < 4, upper, lower)
            ref[2 * zz + 1, XL:XE] = pltpu.roll(jnp.where(sub8 < 4, lower, upper), 4, 0)

    drains.pop("own")()
    conc = ((1, em), (2, es))
    for f, ref in conc:
        for c in halo_copies(f, ref, (0, 1)):
            c.start()
    drains["c01"] = lambda: [c.wait() for f, ref in conc for c in halo_copies(f, ref, (0, 1))]
    for f, ref in conc:
        pack_rows(f, ref)
    ev[0:32] = vent[...].astype(F32)
    vent_copies = [
        pltpu.make_async_remote_copy(
            src_ref=ev.at[pl.ds(24, 8)], dst_ref=vin.at[0],
            send_sem=vs.at[0], recv_sem=vq.at[0], device_id=dev(h_up, d)),
        pltpu.make_async_remote_copy(
            src_ref=ev.at[pl.ds(0, 8)], dst_ref=vin.at[1],
            send_sem=vs.at[1], recv_sem=vq.at[1], device_id=dev(h_dn, d)),
    ]

    def table(z, _):
        khs[z] = ph[layer[z]]
        return 0

    lax.fori_loop(0, NZ, table, 0)
    cpl[0] = 0.0
    cpl[NZ] = 0.0

    def face(i, _):
        a, c = pv[layer[i - 1]], pv[layer[i]]
        cpl[i] = 2.0 * a * c / (a + c)
        return 0

    lax.fori_loop(1, NZ, face, 0)

    lam = eig_x[...] + jnp.concatenate([ey[...]] * 4, axis=1)
    blank = jnp.zeros((16, N), F32)
    state = (blank, blank)
    for j in range(NX_CHIPS):
        def factor(i, carry, j=j):
            rd, ru, bd, bu = carry
            z, y = ZB * j + i, NZ - 1 - ZB * j - i
            cu, cd = cpl[z], cpl[z + 1]
            v = 1.0 / ((cu + cd + khs[z] * lam + STORAGE) - cu * rd)
            inv_d[z] = v
            rd, bd = cd * v, bd * (cu * v)
            cu, cd = cpl[y], cpl[y + 1]
            v = 1.0 / ((cu + cd + khs[y] * lam + STORAGE) - cd * ru)
            inv_u[y] = v
            ru, bu = cu * v, bu * (cd * v)
            return rd, ru, bd, bu

        rd, ru, bd, bu = lax.fori_loop(0, ZB, factor, state + (blank + 1.0, blank + 1.0))
        state = (rd, ru)
        prod_d[j] = bd
        prod_u[NX_CHIPS - 1 - j] = bu
    base = ZB * chip

    def product(i, v):
        v = v * (cpl[base + i] * inv_d[base + i])
        pi[i] = v
        return v

    lax.fori_loop(0, ZB, product, blank + 1.0)
    r_last = cpl[base + ZB] * inv_d[base + ZB - 1]
    r_next = cpl[base + ZB] * inv_u[jnp.minimum(base + ZB, NZ - 1)]
    join = 1.0 / (1.0 - r_last * r_next)

    r1[slot(q)] = y1[q]

    for j in range(NQ - 1):
        copy1(j, fellow(j, -1)[0]).wait_recv()
    for f, ref in conc:
        for c in halo_copies(f, ref, range(2, 8)):
            c.start()
    for c in vent_copies:
        c.start()
    drains["c28"] = lambda: [c.wait() for c in vent_copies + [c for f, ref in conc for c in halo_copies(f, ref, range(2, 8))]]

    group = lax.broadcasted_iota(jnp.int32, (16, 128), 1) // 32

    def regroup(v):
        lower, even = group < 2, lax.rem(group, 2) == 0
        p = [jnp.where(lower, v[i], pltpu.roll(v[i + 2], 64, 1)) for i in range(2)]
        r = [jnp.where(lower, pltpu.roll(v[i], 64, 1), v[i + 2]) for i in range(2)]
        out = []
        for a, b in (p, r):
            out.append(jnp.where(even, a, pltpu.roll(b, 32, 1)))
            out.append(jnp.where(even, pltpu.roll(a, 96, 1), b))
        return out

    for c in range(2):
        for g in range(2):
            for t in range(4):
                v = regroup([r1[NH * c + 4 * t + i, :, 128 * g:128 * g + 128] for i in range(4)])
                for i in range(4):
                    row = 16 * (8 * c + 4 * g + i)
                    hi, lo = split(v[i])
                    ah[row:row + 16, 128 * t:128 * t + 128] = hi
                    al[row:row + 16, 128 * t:128 * t + 128] = lo
    for n in range(2):
        cols = (hhi[:, 256 * n:256 * n + 256], hlo[:, 256 * n:256 * n + 256])
        o = dot3((ah[...], al[...]), cols)
        fz[:, :, 256 * n:256 * n + 256] = (o * (1.0 / (N * N))).reshape(ZB, 16, 256)

    def down(i, v):
        k = inv_d[base + i]
        v = fz[i] * k + (cpl[base + i] * k) * v
        gd[i] = v
        return v

    def upward(n, v):
        i = ZB - 1 - n
        k = inv_u[base + i]
        return fz[i] * k + (cpl[base + i + 1] * k) * v

    send_a[0] = lax.fori_loop(0, ZB, down, blank, unroll=4)
    send_a[1] = lax.fori_loop(0, ZB, upward, blank, unroll=4)

    def copy2(j, origin):
        to = lax.rem(chip + j, NX_CHIPS)
        return pltpu.make_async_remote_copy(
            src_ref=send_a.at[jnp.where(to > chip, 0, 1)], dst_ref=recv_a.at[origin],
            send_sem=s2.at[j], recv_sem=q2.at[j], device_id=dev(h, 2 * to + core))

    def go2(j, _):
        copy2(j, chip).start()
        return 0

    lax.fori_loop(1, NX_CHIPS, go2, 0)

    def left2(j, _):
        copy2(j, chip).wait_send()
        return 0

    drains["2"] = lambda: lax.fori_loop(1, NX_CHIPS, left2, 0)
    recv_a[chip] = blank

    def done2(j, _):
        copy2(j, lax.rem(chip + NX_CHIPS - j, NX_CHIPS)).wait_recv()
        return 0

    lax.fori_loop(1, NX_CHIPS, done2, 0)
    from_top, from_bottom = blank, blank
    for j in range(NX_CHIPS - 1):
        from_top = jnp.where(j < chip, recv_a[j] + prod_d[j] * from_top, from_top)
        k = NX_CHIPS - 1 - j
        from_bottom = jnp.where(k > chip, recv_a[k] + prod_u[k] * from_bottom, from_bottom)

    def solved(i, p):
        row = pl.ds(pl.multiple_of(16 * i, 16), 16)
        hi, lo = split(p)
        ah[row, :] = hi
        al[row, :] = lo

    p = (gd[ZB - 1] + pi[ZB - 1] * from_top + r_last * from_bottom) * join
    solved(ZB - 1, p)

    def up(n, p):
        i = ZB - 2 - n
        p = gd[i] + pi[i] * from_top + (cpl[base + i + 1] * inv_d[base + i]) * p
        solved(i, p)
        return p

    lax.fori_loop(0, ZB - 1, up, p)
    for n in range(2):
        cols = (hhi[:, 256 * n:256 * n + 256], hlo[:, 256 * n:256 * n + 256])
        fz[:, :, 256 * n:256 * n + 256] = dot3((ah[...], al[...]), cols).reshape(ZB, 16, 256)
    for c in range(2):
        for g in range(2):
            for t in range(4):
                v = regroup([fz[8 * c + 4 * g + i, :, 128 * t:128 * t + 128] for i in range(4)])
                for i in range(4):
                    w1[NH * c + 4 * t + i, :, 128 * g:128 * g + 128] = v[i]

    def copy4(j, oq):
        pq, fh, fc = fellow(j)
        return pltpu.make_async_remote_copy(
            src_ref=w1.at[slot(pq)], dst_ref=y4.at[oq],
            send_sem=s4.at[j], recv_sem=q4.at[j], device_id=dev(fh, 2 * chip + fc))

    def go4():
        for j in range(NQ - 1):
            copy4(j, q).start()

    go4()

    def left4():
        for j in range(NQ - 1):
            copy4(j, q).wait_send()

    drains["4"] = left4
    y4[q] = w1[slot(q)]

    del drains["c01"], drains["c28"]
    for f, ref in conc:
        for c in halo_copies(f, ref, range(8)):
            c.wait()
        unpack_rows(f, ref)
    for c in vent_copies:
        c.wait()
    ev[XL:XE] = jnp.where(sub8 < 4, vin[1], vin[0])

    for j in range(NQ - 1):
        copy4(j, fellow(j, -1)[0]).wait_recv()

    s = split(y4[...].reshape(N, ZL * XL).T)
    for n in range(2):
        o = dot3(s, (hhi[:, 256 * n:256 * n + 256], hlo[:, 256 * n:256 * n + 256]))
        ep[HALO:HALO + ZL, 0:32, 256 * n:256 * n + 256] = o.reshape(ZL, XL, 256)
    outs = [pltpu.make_async_copy(ep.at[pl.ds(HALO, ZL), pl.ds(0, XL)], out_p, lsem.at[8])]
    outs[0].start()
    drains["out"] = lambda: [c.wait() for c in outs]

    near = halo_copies(0, ep, (8, 9, 2, 3))
    rest = halo_copies(0, ep, (10, 11, 4, 5, 6, 7))
    for c in near[:2]:
        c.start()
    pack_rows(0, ep)
    for c in near[2:] + rest:
        c.start()
    drains["p"] = lambda: [c.wait_send() for c in near + rest]
    drains["pr"] = lambda: [c.wait_recv() for c in rest]
    for c in near:
        c.wait_recv()
    unpack_rows(0, ep, (2, 3, 4, 5))

    def cell(i):
        gz = lax.rem(d * ZL + i + (NZ - HALO), NZ)
        kh, cu, cd = khs[gz], cpl[gz], cpl[gz + 1]
        p = ep[i]
        east = -kh * (pltpu.roll(p, XE - 1, 0) - p)
        north = -kh * (pltpu.roll(p, N - 1, 1) - p)
        above = -cu * (p - ep[i - 1])
        below = -cd * (ep[i + 1] - p)
        return east, pltpu.roll(east, 1, 0), north, pltpu.roll(north, 1, 1), above, below

    def speed(i, m):
        e, w, n, s_, a, c = [jnp.abs(v[0:32]) for v in cell(i)]
        v = e + w + n + s_ + a + c
        v = jnp.max(v.reshape(4, 8, N), axis=0)
        return jnp.maximum(m, jnp.maximum(jnp.maximum(v[:, :128], v[:, 128:256]),
                                          jnp.maximum(v[:, 256:384], v[:, 384:])))

    mx[0] = lax.fori_loop(HALO, HALO + ZL, speed, jnp.zeros((8, 128), F32))

    def copy_m(j, origin):
        return pltpu.make_async_remote_copy(
            src_ref=mx.at[0], dst_ref=mxh.at[origin], send_sem=ms.at[j], recv_sem=mq.at[j],
            device_id=dev(mate(j), d))

    def copy_n(j, origin):
        return pltpu.make_async_remote_copy(
            src_ref=mx.at[1], dst_ref=mxd.at[origin], send_sem=ns.at[j], recv_sem=nq.at[j],
            device_id=dev(h, lax.rem(d + j, ND)))

    def go_m(j, _):
        copy_m(j, h).start()
        return 0

    lax.fori_loop(1, NH, go_m, 0)
    def left_m(j, _):
        copy_m(j, h).wait_send()
        return 0
    drains["m"] = lambda: lax.fori_loop(1, NH, left_m, 0)
    mxh[h] = mx[0]

    def stencil(get, c_ref, i):
        c = c_ref[i]
        return (get(0) * c
                + get(1) * pltpu.roll(c, XE - 1, 0) + get(2) * pltpu.roll(c, 1, 0)
                + get(3) * pltpu.roll(c, N - 1, 1) + get(4) * pltpu.roll(c, 1, 1)
                + get(5) * c_ref[i + 1] + get(6) * c_ref[i - 1])

    def tendencies(m_ref, s_ref, i):
        get = lambda k: coef[k, i - 1]
        react = REACTION * m_ref[i] * s_ref[i]
        return (stencil(get, m_ref, i) + (react - VENT_INPUT * ev[...]),
                stencil(get, s_ref, i) + react)

    def prepare(i, _):
        e, w, n, s_, a, c = cell(i)
        pos, neg = (lambda v: jnp.maximum(v, 0.0)), (lambda v: jnp.minimum(v, 0.0))
        coef[0, i - 1] = (pos(e) - neg(w)) + (pos(n) - neg(s_)) + (pos(c) - neg(a))
        coef[1, i - 1] = neg(e)
        coef[2, i - 1] = -pos(w)
        coef[3, i - 1] = neg(n)
        coef[4, i - 1] = -pos(s_)
        coef[5, i - 1] = neg(c)
        coef[6, i - 1] = -pos(a)
        t_m, t_s = tendencies(em, es, i)
        tend[0, i - 1] = t_m
        tend[1, i - 1] = t_s
        return 0

    def bend(i, _):
        get = lambda k: coef[k, i - 1]
        curve[0, i - 2] = stencil(get, tend.at[0], i - 1)
        curve[1, i - 2] = stencil(get, tend.at[1], i - 1)
        return 0

    lax.fori_loop(HALO + 1, HALO + ZL - 1, prepare, 0)
    drains.pop("pr")()
    unpack_rows(0, ep, (0, 1, 6, 7))
    lax.fori_loop(1, HALO + 1, prepare, 0)
    lax.fori_loop(HALO + ZL - 1, ZE - 1, prepare, 0)

    def done_m(j, _):
        copy_m(j, lax.rem(h + NH - j, NH)).wait_recv()
        return 0

    lax.fori_loop(1, NH, done_m, 0)
    mx[1] = jnp.max(mxh[...], axis=0)

    def go_n(j, _):
        copy_n(j, d).start()
        return 0

    lax.fori_loop(1, ND, go_n, 0)
    def left_n(j, _):
        copy_n(j, d).wait_send()
        return 0
    drains["n"] = lambda: lax.fori_loop(1, ND, left_n, 0)
    mxd[d] = mx[1]

    lax.fori_loop(2, ZE - 2, bend, 0)

    def done_n(j, _):
        copy_n(j, lax.rem(d + ND - j, ND)).wait_recv()
        return 0

    lax.fori_loop(1, ND, done_n, 0)
    fastest = jnp.max(jnp.max(mxd[...], axis=0), axis=(0, 1), keepdims=True)
    dt = COURANT / (fastest + 1e-6)

    def first(i, _):
        m, s, t_m, t_s = em[i], es[i], tend[0, i - 1], tend[1, i - 1]
        m1, s1 = m - dt * t_m, s - dt * t_s
        more = REACTION * (m1 * s1) - REACTION * (m * s)
        em2[i] = m1 - dt * ((t_m + more) - dt * curve[0, i - 2])
        es2[i] = s1 - dt * ((t_s + more) - dt * curve[1, i - 2])
        return 0

    lax.fori_loop(2, ZE - 2, first, 0)

    def step(a, c, lo):
        def body(i, _):
            t_m, t_s = tendencies(a[0], a[1], i)
            c[0][i] = a[0][i] - dt * t_m
            c[1][i] = a[1][i] - dt * t_s
            return 0

        lax.fori_loop(lo, ZE - lo, body, 0)

    step((em2, es2), (em, es), 3)

    def last(i, _):
        t_m, t_s = tendencies(em, es, i)
        res_m[i - HALO] = (em[i] - dt * t_m)[0:32]
        res_s[i - HALO] = (es[i] - dt * t_s)[0:32]
        return 0

    for part in range(2):
        half = ZL // 2
        lax.fori_loop(HALO + half * part, HALO + half * (part + 1), last, 0)
        at = pl.ds(half * part, half)
        for k, (ref, out) in enumerate(((res_m, out_m), (res_s, out_s))):
            outs.append(pltpu.make_async_copy(ref.at[at], out.at[at], lsem.at[9 + 2 * part + k]))
            outs[-1].start()
    for f in drains.values():
        f()


def deliver(*refs):
    ins, outs, (buf, sem_in, sem_out) = refs[:3], refs[3:6], refs[6:]
    part = ZL // PARTS
    moves = []
    for k in range(3):
        for n in range(PARTS):
            at = pl.ds(n * part, part)
            moves.append((
                pltpu.make_async_copy(ins[k].at[at], buf.at[k, at], sem_in.at[k, n]),
                pltpu.make_async_copy(buf.at[k, at], outs[k].at[at], sem_out.at[k, n])))
    for a, _ in moves:
        a.start()
    for a, b in moves:
        a.wait()
        b.start()
    for _, b in moves:
        b.wait()


def local(source_field, methane, sulfate, layer_of_cell, perm_horizontal, perm_vertical, vent_mask):
    hi, lo, eig_x, eig_y = tables()
    smem = pl.BlockSpec(memory_space=pltpu.SMEM)
    hbm = pl.BlockSpec(memory_space=pl.ANY)
    field = jax.ShapeDtypeStruct((ZL, XL, N), F32)
    dma = pltpu.SemaphoreType.DMA
    ext = pltpu.VMEM((ZE, XE, N), F32)
    scratch = [
        pltpu.VMEM((ZL, XL, N), F32),
        pltpu.VMEM((XL, N), jnp.int32),
        pltpu.VMEM((N, N), BF16),
        pltpu.VMEM((N, N), BF16),
        pltpu.VMEM((16, N), F32),
        pltpu.VMEM((ZL, XL, N), F32),
        pltpu.VMEM((ZL, XL, N), F32),
        pltpu.VMEM((NQ, 16, ZL * XL), F32),
        pltpu.VMEM((NQ, 16, ZL * XL), F32),
        pltpu.VMEM((ZB * 16, N), BF16),
        pltpu.VMEM((ZB * 16, N), BF16),
        pltpu.VMEM((ZB, 16, N), F32),
        pltpu.VMEM((NQ, 16, ZL * XL), F32),
        pltpu.VMEM((NQ, 16, ZL * XL), F32),
        pltpu.VMEM((16, 128), F32),
        pltpu.VMEM((NZ, 16, N), F32),
        pltpu.VMEM((NZ, 16, N), F32),
        pltpu.VMEM((NX_CHIPS, 16, N), F32),
        pltpu.VMEM((NX_CHIPS, 16, N), F32),
        pltpu.VMEM((ZB, 16, N), F32),
        pltpu.VMEM((ZB, 16, N), F32),
        pltpu.VMEM((2, 16, N), F32),
        pltpu.VMEM((NX_CHIPS, 16, N), F32),
        ext, ext, ext, ext, ext,
        pltpu.VMEM((XE, N), F32),
        pltpu.VMEM((2, 8, N), F32),
        pltpu.VMEM((3, 2, ZL // 2, 8, N), F32),
        pltpu.VMEM((3, 2, ZE // 2, 8, N), F32),
        pltpu.VMEM((7, ZE - 2, XE, N), F32),
        pltpu.VMEM((2, ZE - 2, XE, N), F32),
        pltpu.VMEM((2, ZE - 4, XE, N), F32),
        pltpu.VMEM((2, 8, 128), F32),
        pltpu.VMEM((NH, 8, 128), F32),
        pltpu.VMEM((ND, 8, 128), F32),
        pltpu.SMEM((NZ + 1,), F32),
        pltpu.SMEM((NZ,), F32),
        dma((NQ,)), dma((NQ,)), dma((NX_CHIPS,)), dma((NX_CHIPS,)), dma((NQ,)), dma((NQ,)),
        dma((3, 12)), dma((3, 12)), dma((2,)), dma((2,)),
        dma((NH,)), dma((NH,)), dma((ND,)), dma((ND,)), dma((13,)),
    ]
    results = pl.pallas_call(
        kernel,
        out_shape=(field, field, field),
        in_specs=[hbm, hbm, hbm, smem, smem, smem, hbm, hbm, hbm, hbm, hbm],
        out_specs=(hbm, hbm, hbm),
        scratch_shapes=scratch,
        compiler_params=pltpu.CompilerParams(
            collective_id=0, has_side_effects=True, vmem_limit_bytes=60 * 1024 * 1024),
    )(source_field, methane, sulfate, layer_of_cell, perm_horizontal, perm_vertical, vent_mask,
      jnp.asarray(hi), jnp.asarray(lo), jnp.asarray(eig_x), jnp.asarray(eig_y))
    return pl.pallas_call(
        deliver,
        out_shape=(field, field, field),
        in_specs=[hbm] * 3,
        out_specs=(hbm,) * 3,
        scratch_shapes=[pltpu.VMEM((3, ZL, XL, N), F32), dma((3, PARTS)), dma((3, PARTS))],
    )(*results)


def solution(mesh):
    field = P("depth", "horiz", None)
    return jax.shard_map(
        local,
        mesh=mesh,
        in_specs=(field, field, field, P(), P(), P(), P("horiz", None)),
        out_specs=(field, field, field),
        check_vma=False,
    )
```

profile of v0, /device:TPU:1, one launch (start us, length us, event | category | flops | bytes accessed | tf_op | source)
XLA Modules:
  0.0 59.5 jit_solution(14493586774465694145)
XLA Ops:
  0.6 56.7 %shard_map.130 = (f32[8,32,512]{2,1,0:T(8,128)}, f32[8,32,512]{2,1,0:T(8,128)}, f32[8,32,512]{2,1,0:T(8,128)}) custom-call(f32[8,32,512]{2,1,0:T(8,128)} %src_in.1, f32[8,32,512]{2,1,0:T(8,128)} %met.1, f32[8,32,512]{2,1,0:T(8,128)} %sul.1, s32[64]{0:T(128)} %layer.1, f32[8]{0:T(128)} %ph.1, f32[8]{0:T(128)} %pv.1, s32[32,512]{1,0:T(8,128)} %vent_in.1, ...), custom_call_target="tpu_custom_call" | custom-call | tf_op jit(solution)/shard_map/pallas_call | solution.py:635
  57.3 2.2 %shard_map.131 = (f32[8,32,512]{2,1,0:T(8,128)}, f32[8,32,512]{2,1,0:T(8,128)}, f32[8,32,512]{2,1,0:T(8,128)}) custom-call(f32[8,32,512]{2,1,0:T(8,128)} %get-tuple-element.6.refs_0_, f32[8,32,512]{2,1,0:T(8,128)} %get-tuple-element.7.refs_1_, f32[8,32,512]{2,1,0:T(8,128)} %get-tuple-element.8.refs_2_), custom_call_target="tpu_custom_call" | custom-call | tf_op jit(solution)/shard_map/pallas_call | solution.py:645
where the time goes:
time: 59.7 us; the launch traced here: 59.5 us
  Pallas kernels  58.9 us (99%)
  between operations  0.64 us (1%)
    pallas_call x1, Pallas kernels, local(): pl.pallas_call(kernel, out_shape=(field, field, field), in_specs=[hbm, hb...  56.7 us
    pallas_call x1, Pallas kernels, local(): pl.pallas_call(deliver, out_shape=(field, field, field), in_specs=[hbm] *...  2.19 us

commit v1 on v0

--- a/solution.py
+++ b/solution.py
@@ -60,9 +60,9 @@
 
 
 def kernel(
-    src_in, met, sul, layer, ph, pv, vent_in, hhi_in, hlo_in, eig_x_in, eig_y,
+    src_in, met, sul, layer_in, ph_in, pv_in, vent_in, hhi_in, hlo_in, eig_x_in, eig_y,
     out_p, out_m, out_s,
-    src, vent, hhi, hlo, eig_x, res_m, res_s,
+    src, vent, hhi, hlo, eig_x, res_m, res_s, layer, ph, pv,
     y1, r1, ah, al, fz, w1, y4, ey,
     inv_d, inv_u, prod_d, prod_u, gd, pi, send_a, recv_a,
     ep, em, es, em2, es2, ev, vin, pack, xin, coef, tend, curve,
@@ -126,6 +126,9 @@
         pltpu.make_async_copy(eig_y.at[q], ey, lsem.at[2]),
         pltpu.make_async_copy(vent_in, vent, lsem.at[6]),
         pltpu.make_async_copy(eig_x_in, eig_x, lsem.at[7]),
+        pltpu.make_async_copy(layer_in, layer, lsem.at[13]),
+        pltpu.make_async_copy(ph_in, ph, lsem.at[14]),
+        pltpu.make_async_copy(pv_in, pv, lsem.at[15]),
     ]
     for c in own_copies:
         c.start()
@@ -262,7 +265,7 @@
 
     r1[slot(q)] = y1[q]
 
-    for j in range(NQ - 1):
+    for j in range(8):
         copy1(j, fellow(j, -1)[0]).wait_recv()
     for f, ref in conc:
         for c in halo_copies(f, ref, range(2, 8)):
@@ -271,6 +274,8 @@
         c.start()
     drains["c28"] = lambda: [c.wait() for c in vent_copies + [c for f, ref in conc for c in halo_copies(f, ref, range(2, 8))]]
 
+    for j in range(8, NQ - 1):
+        copy1(j, fellow(j, -1)[0]).wait_recv()
     group = lax.broadcasted_iota(jnp.int32, (16, 128), 1) // 32
 
     def regroup(v):
@@ -317,11 +322,8 @@
             src_ref=send_a.at[jnp.where(to > chip, 0, 1)], dst_ref=recv_a.at[origin],
             send_sem=s2.at[j], recv_sem=q2.at[j], device_id=dev(h, 2 * to + core))
 
-    def go2(j, _):
+    for j in (2, 1, 3):
         copy2(j, chip).start()
-        return 0
-
-    lax.fori_loop(1, NX_CHIPS, go2, 0)
 
     def left2(j, _):
         copy2(j, chip).wait_send()
@@ -415,10 +417,6 @@
         c.start()
     drains["p"] = lambda: [c.wait_send() for c in near + rest]
     drains["pr"] = lambda: [c.wait_recv() for c in rest]
-    for c in near:
-        c.wait_recv()
-    unpack_rows(0, ep, (2, 3, 4, 5))
-
     def cell(i):
         gz = lax.rem(d * ZL + i + (NZ - HALO), NZ)
         kh, cu, cd = khs[gz], cpl[gz], cpl[gz + 1]
@@ -429,14 +427,27 @@
         below = -cd * (ep[i + 1] - p)
         return east, pltpu.roll(east, 1, 0), north, pltpu.roll(north, 1, 1), above, below
 
-    def speed(i, m):
-        e, w, n, s_, a, c = [jnp.abs(v[0:32]) for v in cell(i)]
-        v = e + w + n + s_ + a + c
-        v = jnp.max(v.reshape(4, 8, N), axis=0)
-        return jnp.maximum(m, jnp.maximum(jnp.maximum(v[:, :128], v[:, 128:256]),
-                                          jnp.maximum(v[:, 256:384], v[:, 384:])))
-
-    mx[0] = lax.fori_loop(HALO, HALO + ZL, speed, jnp.zeros((8, 128), F32))
+    def speed(*rows):
+        def body(i, m):
+            e, w, n, s_, a, c = [jnp.abs(v) for v in cell(i)]
+            v = e + w + n + s_ + a + c
+            for r in rows:
+                for k in range(0, N, 128):
+                    m = jnp.maximum(m, v[r:r + 8, k:k + 128])
+            return m
+
+        return body
+
+    inner = (HALO + 1, HALO + ZL - 1)
+    m = lax.fori_loop(*inner, speed(8, 16), jnp.zeros((8, 128), F32))
+    for c in near:
+        c.wait_recv()
+    unpack_rows(0, ep, (2, 3, 4, 5))
+
+    m = lax.fori_loop(*inner, speed(0, 24), m)
+    for i in (HALO, HALO + ZL - 1):
+        m = speed(0, 8, 16, 24)(i, m)
+    mx[0] = m
 
     def copy_m(j, origin):
         return pltpu.make_async_remote_copy(
@@ -586,7 +597,6 @@
 
 def local(source_field, methane, sulfate, layer_of_cell, perm_horizontal, perm_vertical, vent_mask):
     hi, lo, eig_x, eig_y = tables()
-    smem = pl.BlockSpec(memory_space=pltpu.SMEM)
     hbm = pl.BlockSpec(memory_space=pl.ANY)
     field = jax.ShapeDtypeStruct((ZL, XL, N), F32)
     dma = pltpu.SemaphoreType.DMA
@@ -599,6 +609,9 @@
         pltpu.VMEM((16, N), F32),
         pltpu.VMEM((ZL, XL, N), F32),
         pltpu.VMEM((ZL, XL, N), F32),
+        pltpu.SMEM((NZ,), jnp.int32),
+        pltpu.SMEM((8,), F32),
+        pltpu.SMEM((8,), F32),
         pltpu.VMEM((NQ, 16, ZL * XL), F32),
         pltpu.VMEM((NQ, 16, ZL * XL), F32),
         pltpu.VMEM((ZB * 16, N), BF16),
@@ -630,12 +643,12 @@
         pltpu.SMEM((NZ,), F32),
         dma((NQ,)), dma((NQ,)), dma((NX_CHIPS,)), dma((NX_CHIPS,)), dma((NQ,)), dma((NQ,)),
         dma((3, 12)), dma((3, 12)), dma((2,)), dma((2,)),
-        dma((NH,)), dma((NH,)), dma((ND,)), dma((ND,)), dma((13,)),
+        dma((NH,)), dma((NH,)), dma((ND,)), dma((ND,)), dma((16,)),
     ]
     results = pl.pallas_call(
         kernel,
         out_shape=(field, field, field),
-        in_specs=[hbm, hbm, hbm, smem, smem, smem, hbm, hbm, hbm, hbm, hbm],
+        in_specs=[hbm] * 11,
         out_specs=(hbm, hbm, hbm),
         scratch_shapes=scratch,
         compiler_params=pltpu.CompilerParams(

time: 59.7 us -> 57.6 us (0.965)
  Pallas kernels: 58.9 us -> 56.8 us
    pallas_call x1, Pallas kernels: 56.7 us -> 54.6 us  [local(): pl.pallas_call(kernel, out_shape=(field, field, field), in_specs=[hbm] *...]
where the time goes in v1:
time: 57.6 us; the launch traced here: 57.4 us
  Pallas kernels  56.8 us (99%)
  between operations  0.64 us (1%)
    pallas_call x1, Pallas kernels, local(): pl.pallas_call(kernel, out_shape=(field, field, field), in_specs=[hbm] *...  54.6 us
    pallas_call x1, Pallas kernels, local(): pl.pallas_call(deliver, out_shape=(field, field, field), in_specs=[hbm] *...  2.19 us

profile of v1, /device:TPU:1, one launch (start us, length us, event | category | flops | bytes accessed | tf_op | source)
XLA Modules:
  0.0 57.4 jit_solution(11647090275644757418)
XLA Ops:
  0.6 54.6 %shard_map.130 = (f32[8,32,512]{2,1,0:T(8,128)}, f32[8,32,512]{2,1,0:T(8,128)}, f32[8,32,512]{2,1,0:T(8,128)}) custom-call(f32[8,32,512]{2,1,0:T(8,128)} %src_in.1, f32[8,32,512]{2,1,0:T(8,128)} %met.1, f32[8,32,512]{2,1,0:T(8,128)} %sul.1, s32[64]{0:T(128)} %layer_in.1, f32[8]{0:T(128)} %ph_in.1, f32[8]{0:T(128)} %pv_in.1, s32[32,512]{1,0:T(8,128)} %vent_in.1, ...), custom_call_target="tpu_custom_call" | custom-call | tf_op jit(solution)/shard_map/pallas_call | solution.py:648
  55.3 2.2 %shard_map.131 = (f32[8,32,512]{2,1,0:T(8,128)}, f32[8,32,512]{2,1,0:T(8,128)}, f32[8,32,512]{2,1,0:T(8,128)}) custom-call(f32[8,32,512]{2,1,0:T(8,128)} %get-tuple-element.6.refs_0_, f32[8,32,512]{2,1,0:T(8,128)} %get-tuple-element.7.refs_1_, f32[8,32,512]{2,1,0:T(8,128)} %get-tuple-element.8.refs_2_), custom_call_target="tpu_custom_call" | custom-call | tf_op jit(solution)/shard_map/pallas_call | solution.py:658

commit v2 on v1

--- a/solution.py
+++ b/solution.py
@@ -529,6 +529,9 @@
     mxd[d] = mx[1]
 
     lax.fori_loop(2, ZE - 2, bend, 0)
+
+    for key in ("1", "2", "4", "p", "m"):
+        drains.pop(key)()
 
     def done_n(j, _):
         copy_n(j, lax.rem(d + ND - j, ND)).wait_recv()

time: 57.6 us -> 57.5 us (level)
  no operation moved by 1% of the time
where the time goes in v2:
time: 57.5 us; the launch traced here: 57.3 us
  Pallas kernels  56.7 us (99%)
  between operations  0.64 us (1%)
    pallas_call x1, Pallas kernels, local(): pl.pallas_call(kernel, out_shape=(field, field, field), in_specs=[hbm] *...  54.5 us
    pallas_call x1, Pallas kernels, local(): pl.pallas_call(deliver, out_shape=(field, field, field), in_specs=[hbm] *...  2.19 us

profile of v2, /device:TPU:1, one launch (start us, length us, event | category | flops | bytes accessed | tf_op | source)
XLA Modules:
  0.0 57.3 jit_solution(5820055693826938325)
XLA Ops:
  0.6 54.5 %shard_map.130 = (f32[8,32,512]{2,1,0:T(8,128)}, f32[8,32,512]{2,1,0:T(8,128)}, f32[8,32,512]{2,1,0:T(8,128)}) custom-call(f32[8,32,512]{2,1,0:T(8,128)} %src_in.1, f32[8,32,512]{2,1,0:T(8,128)} %met.1, f32[8,32,512]{2,1,0:T(8,128)} %sul.1, s32[64]{0:T(128)} %layer_in.1, f32[8]{0:T(128)} %ph_in.1, f32[8]{0:T(128)} %pv_in.1, s32[32,512]{1,0:T(8,128)} %vent_in.1, ...), custom_call_target="tpu_custom_call" | custom-call | tf_op jit(solution)/shard_map/pallas_call | solution.py:651
  55.1 2.2 %shard_map.131 = (f32[8,32,512]{2,1,0:T(8,128)}, f32[8,32,512]{2,1,0:T(8,128)}, f32[8,32,512]{2,1,0:T(8,128)}) custom-call(f32[8,32,512]{2,1,0:T(8,128)} %get-tuple-element.6.refs_0_, f32[8,32,512]{2,1,0:T(8,128)} %get-tuple-element.7.refs_1_, f32[8,32,512]{2,1,0:T(8,128)} %get-tuple-element.8.refs_2_), custom_call_target="tpu_custom_call" | custom-call | tf_op jit(solution)/shard_map/pallas_call | solution.py:661
